TPU v7x, 1024 devices: a whole 4x8x16 slice. The times are simulated.
1024 devices in a mesh: section: 16 (over z_hi, y), expert: 64 (over z_lo, x, core).
Axes of the slice: x: 4, y: 8, z: 16 (z_hi: 2, z_lo: 8; z = z_hi * 8 + z_lo), core: 2. Of those that a mesh axis runs over, the one named last changes fastest.
Arguments:
- route_ids: int32 [1, 16, 4096, 1], P(None, 'section', 'expert'), may hold values from 0 to 15; in each aligned block of 64 rows (0 to 63, 64 to 127, ..., all dimensions but the last counted through in order) at most 8 rows name the same one
- route_probs: float32 [1, 16, 4096, 1], P(None, 'section', 'expert'), may hold values from 0.2 to 1
- checkpoints: bfloat16 [1, 16, 4096, 2048], P(None, 'section', 'expert'), may hold values from -6 to 6
- grad_in: bfloat16 [16, 4096, 2048], P('section', 'expert'), may hold values from -6 to 6
- gate_weight: bfloat16 [16, 2048, 12288], P('section', None, 'expert'), may hold values from -0.125 to 0.125
- up_weight: bfloat16 [16, 2048, 12288], P('section', None, 'expert'), may hold values from -0.125 to 0.125
- down_weight: bfloat16 [16, 12288, 2048], P('section', 'expert'), may hold values from -0.21875 to 0.21875
Outputs:
- grad_out: bfloat16 [16, 4096, 2048], P('section', 'expert')
Inputs may be any that keep to these rules, and one draw needn't show every extreme that they name: `route_ids`: each token names 1 different experts. In each aligned block of 64 tokens of one step and section (the tokens of one device) no expert is named by more than 8 tokens, and in some block one expert is named by exactly 8.
All inputs are finite; a program needn't handle non-finite values.
Results may differ from a plain program's by a relative error of at most 0.0042.
Values may be sent and summed in bfloat16 or wider, within the bound.
A program may use at most 32 MiB of HBM per device.

v0:
```python
import jax
import jax.numpy as jnp
from jax import lax
from jax.sharding import PartitionSpec as P

SPLIT = 4


def passed_along(shard, axis, by):
    count = lax.axis_size(axis)
    return lax.ppermute(shard, axis, [(i, (i + by) % count) for i in range(count)])


def routing_tables(block_ids, block_probs, experts_live, capacity):
    tokens_here, top_width = block_ids.shape
    pair_ids = block_ids.reshape(-1)
    onehot = (pair_ids[:, None] == jnp.arange(experts_live, dtype=jnp.int32)[None, :]).astype(
        jnp.int32
    )
    earlier = jnp.cumsum(onehot, axis=0) - onehot
    slot_index = jnp.sum(earlier * onehot, axis=1).reshape(tokens_here, top_width)
    target = block_ids * capacity + slot_index
    select = (
        target[:, :, None] == jnp.arange(experts_live * capacity, dtype=jnp.int32)[None, None, :]
    ).astype(jnp.float32)
    placing = jnp.sum(select, axis=1)
    weighting = jnp.sum(block_probs[:, :, None] * select, axis=1)
    return (placing, weighting)


def pack_rows(placing, rows):
    return lax.dot_general(
        placing.astype(jnp.bfloat16),
        rows,
        (((0,), (0,)), ((), ())),
        preferred_element_type=jnp.float32,
    ).astype(jnp.bfloat16)


def spread_rows(packed, experts_live, capacity, share_count):
    feature_width = packed.shape[1]
    spread = jnp.broadcast_to(
        packed.reshape(experts_live, 1, capacity, feature_width),
        (experts_live, share_count, capacity, feature_width),
    )
    return spread.reshape(experts_live * share_count, capacity, feature_width)


def combine_rows(returned, weighting, grad_rows, experts_live, share_count, capacity):
    feature_width = returned.shape[2]
    summed = jnp.sum(
        returned.reshape(experts_live, share_count, capacity, feature_width).astype(jnp.float32),
        axis=1,
    )
    summed = summed.reshape(experts_live * capacity, feature_width)
    update = grad_rows.astype(jnp.float32) + jnp.dot(
        weighting, summed, precision=lax.Precision.HIGHEST, preferred_element_type=jnp.float32
    )
    return update.astype(jnp.bfloat16)


def share_backward(rows_in, rows_grad, gate_share, up_share, down_share):
    contract = (((1,), (1,)), ((), ()))
    pre_gate = jnp.dot(rows_in, gate_share, preferred_element_type=jnp.float32)
    pre_up = jnp.dot(rows_in, up_share, preferred_element_type=jnp.float32)
    hidden_grad = lax.dot_general(
        rows_grad, down_share, contract, preferred_element_type=jnp.float32
    )
    sigmoid_gate = jax.nn.sigmoid(pre_gate)
    gate_coef = (
        hidden_grad * pre_up * sigmoid_gate * (1.0 + pre_gate * (1.0 - sigmoid_gate))
    ).astype(jnp.bfloat16)
    up_coef = (hidden_grad * pre_gate * sigmoid_gate).astype(jnp.bfloat16)
    total = lax.dot_general(gate_coef, gate_share, contract, preferred_element_type=jnp.float32)
    total = total + lax.dot_general(up_coef, up_share, contract, preferred_element_type=jnp.float32)
    return total.astype(jnp.bfloat16)


def local(route_ids, route_probs, checkpoints, grad_in, gate_weight, up_weight, down_weight):
    devices = lax.axis_size("expert")
    experts_live = devices // SPLIT
    tokens_here = route_ids.shape[2]
    top_width = route_ids.shape[3]
    bucket = 2 * SPLIT * experts_live
    capacity = min(
        tokens_here, max(SPLIT, SPLIT * ((3 * tokens_here * top_width + bucket - 1) // bucket))
    )
    feature_width = checkpoints.shape[3]
    gate_share = gate_weight[0]
    up_share = up_weight[0]
    down_share = down_weight[0]
    grad_rows = grad_in[0]
    placing, weighting = routing_tables(route_ids[0, 0], route_probs[0, 0], experts_live, capacity)
    rows_packed = pack_rows(placing, checkpoints[0, 0])
    grad_packed = pack_rows(placing, grad_rows)
    rows_in = lax.all_to_all(
        spread_rows(rows_packed, experts_live, capacity, SPLIT),
        "expert",
        split_axis=0,
        concat_axis=0,
        tiled=True,
    )
    rows_grad = lax.all_to_all(
        spread_rows(grad_packed, experts_live, capacity, SPLIT),
        "expert",
        split_axis=0,
        concat_axis=0,
        tiled=True,
    )
    share_out = share_backward(
        rows_in.reshape(-1, feature_width),
        rows_grad.reshape(-1, feature_width),
        gate_share,
        up_share,
        down_share,
    )
    partial_rows = share_out.reshape(devices, capacity, feature_width)
    returned = lax.all_to_all(partial_rows, "expert", split_axis=0, concat_axis=0, tiled=True)
    update = combine_rows(returned, weighting, grad_rows, experts_live, SPLIT, capacity)
    grad_rows = passed_along(update, "section", -1)
    return grad_rows[None]


def solution(mesh):
    placed = (
        P(None, "section", "expert", None),
        P(None, "section", "expert", None),
        P(None, "section", "expert", None),
        P("section", "expert", None),
        P("section", None, "expert"),
        P("section", None, "expert"),
        P("section", "expert", None),
    )
    return jax.shard_map(
        local, mesh=mesh, in_specs=placed, out_specs=P("section", "expert", None), check_vma=False
    )
```

profile of v0, /device:TPU:60, one launch (start us, length us, event | category | flops | bytes accessed | tf_op | source)
XLA Modules:
  0.0 381.5 jit_solution(8735019871190080973)
XLA Ops:
  0.0 0.0 copy-start
  0.0 0.8 fusion.41
  0.8 0.1 reduce_window_sum.11
  0.9 0.8 select_reduce_fusion
  1.7 0.7 multiply_add_fusion
  2.4 1.3 fusion.2
  3.7 1.6 broadcast_in_dim.23
  5.4 19.2 %all-to-all-start.1 = ((bf16[64,8,2048]{2,1,0:T(8,128)(2,1)}), bf16[64,8,2048]{2,1,0:T(8,128)(2,1)S(1)}, u32[]{:S(2)}, u32[]{:S(2)}) async-start(bf16[64,8,2048]{2,1,0:T(8,128)(2,1)} %bitcast.11), calls=%async_computation.1 | async-start | bytes 4194304 | tf_op jit(solution)/shard_map/all_to_all | solution.py:96
  24.6 1.3 fusion.1
  25.9 94.9 %all-to-all-done.1 = bf16[64,8,2048]{2,1,0:T(8,128)(2,1)S(1)} async-done(((bf16[64,8,2048]{2,1,0:T(8,128)(2,1)}), bf16[64,8,2048]{2,1,0:T(8,128)(2,1)S(1)}, u32[]{:S(2)}, u32[]{:S(2)}) %all-to-all-start.1) | async-done | bytes 2097184 | tf_op jit(solution)/shard_map/all_to_all | solution.py:96
  120.8 1.6 broadcast_in_dim.21
  122.4 8.2 %all-to-all-start = ((bf16[64,8,2048]{2,1,0:T(8,128)(2,1)}), bf16[64,8,2048]{2,1,0:T(8,128)(2,1)}, u32[]{:S(2)}, u32[]{:S(2)}) async-start(bf16[64,8,2048]{2,1,0:T(8,128)(2,1)} %bitcast.6), calls=%async_computation | async-start | bytes 4194304 | tf_op jit(solution)/shard_map/all_to_all | solution.py:103
  130.6 2.0 fusion.4
  132.6 94.2 %all-to-all-done = bf16[64,8,2048]{2,1,0:T(8,128)(2,1)} async-done(((bf16[64,8,2048]{2,1,0:T(8,128)(2,1)}), bf16[64,8,2048]{2,1,0:T(8,128)(2,1)}, u32[]{:S(2)}, u32[]{:S(2)}) %all-to-all-start) | async-done | bytes 2097184 | tf_op jit(solution)/shard_map/all_to_all | solution.py:103
  226.7 3.4 fusion.8
  230.1 0.0 copy-done
  230.1 4.8 %fusion.23 = f32[512,2048]{1,0:T(8,128)} fusion(f32[512,192]{0,1:T(8,128)} %fusion.8, bf16[64,8,2048]{2,1,0:T(8,128)(2,1)S(1)} %all-to-all-done.1, bf16[1,2048,192]{1,2,0:T(8,128)(2,1)} %param.11, bf16[1,2048,192]{1,2,0:T(8,128)(2,1)S(1)} %copy-done, f32[512,192]{0,1:T(8,128)S(1)} %fusion.4), kind=kOutput, calls=%fused_computation.19 | convolution fusion | flops 806289408 | bytes 8650752 | tf_op jit(solution)/shard_map/dot_general | solution.py:74
  234.9 3.1 fusion
  238.0 104.0 %all_to_all.15 = bf16[64,8,2048]{2,1,0:T(8,128)(2,1)S(1)} all-to-all(bf16[64,8,2048]{2,1,0:T(8,128)(2,1)S(1)} %fusion), channel_id=1, replica_groups=mesh['section'=16,'expert'=64] {'expert'}, dimensions={0} | all-to-all | bytes 4194304 | tf_op jit(solution)/shard_map/all_to_all | solution.py:118
  342.0 0.0 copy-start.1
  342.0 0.0 copy-start.2
  342.0 0.4 convert_reduce_fusion
  342.4 0.6 copy-done.1
  342.9 0.0 copy-done.2
  342.9 0.7 fusion.3
  343.6 3.3 collective-permute-start
  346.9 33.9 %collective-permute-done = bf16[64,2048]{1,0:T(8,128)(2,1)S(1)} collective-permute-done((bf16[64,2048]{1,0:T(8,128)(2,1)S(1)}, bf16[64,2048]{1,0:T(8,128)(2,1)S(1)}, u32[]{:S(2)}, u32[]{:S(2)}) %collective-permute-start) | collective-permute-done | bytes 262176 | tf_op jit(solution)/shard_map/ppermute | solution.py:11
  380.8 0.7 copy.9
Async XLA Ops:
  0.0 230.1 %copy-start = (bf16[1,2048,192]{1,2,0:T(8,128)(2,1)S(1)}, bf16[1,2048,192]{1,2,0:T(8,128)(2,1)}, u32[]{:S(2)}) copy-start(bf16[1,2048,192]{1,2,0:T(8,128)(2,1)} %param.12) | copy-start | bytes 2359300
  5.4 115.5 %all-to-all-start.1 = ((bf16[64,8,2048]{2,1,0:T(8,128)(2,1)}), bf16[64,8,2048]{2,1,0:T(8,128)(2,1)S(1)}, u32[]{:S(2)}, u32[]{:S(2)}) async-start(bf16[64,8,2048]{2,1,0:T(8,128)(2,1)} %bitcast.11), calls=%async_computation.1 | async-start | bytes 4194304 | tf_op jit(solution)/shard_map/all_to_all | solution.py:96
  122.4 104.3 %all-to-all-start = ((bf16[64,8,2048]{2,1,0:T(8,128)(2,1)}), bf16[64,8,2048]{2,1,0:T(8,128)(2,1)}, u32[]{:S(2)}, u32[]{:S(2)}) async-start(bf16[64,8,2048]{2,1,0:T(8,128)(2,1)} %bitcast.6), calls=%async_computation | async-start | bytes 4194304 | tf_op jit(solution)/shard_map/all_to_all | solution.py:103
  342.0 1.0 copy-start.1
  342.0 1.0 copy-start.2
  343.6 37.1 %collective-permute-start = (bf16[64,2048]{1,0:T(8,128)(2,1)S(1)}, bf16[64,2048]{1,0:T(8,128)(2,1)S(1)}, u32[]{:S(2)}, u32[]{:S(2)}) collective-permute-start(bf16[64,2048]{1,0:T(8,128)(2,1)S(1)} %fusion.3), channel_id=1, source_target_pairs={{0,960},{64,0},{128,64},{192,128},{256,192},{320,256},{384,320},{4... | collective-permute-start | bytes 786440 | tf_op jit(solution)/shard_map/ppermute | solution.py:11
where the time goes:
time: 382 us; the launch traced here: 381 us
  waiting for transfers between devices  223 us (58%)
  blocking collectives  104 us (27%)
  starting transfers between devices  30.7 us (8%)
  matrix products  16.6 us (4%)
  local copies, waits for them, and re-layouts  4.46 us (1%)
    all_to_all x1, blocking collectives, local(): lax.all_to_all(partial_rows, 'expert', split_axis=0, concat_axis=0, tiled...  104 us
    all_to_all x1, waiting for transfers between devices, local(): lax.all_to_all(spread_rows(rows_packed, experts_live, capacity, SPLIT), '...  94.9 us
    all_to_all x1, waiting for transfers between devices, local(): lax.all_to_all(spread_rows(grad_packed, experts_live, capacity, SPLIT), '...  94.2 us
    ppermute x1, waiting for transfers between devices, passed_along(): lax.ppermute(shard, axis, [(i, (i + by) % count) for i in range(count)])  33.9 us
    all_to_all x1, starting transfers between devices, local(): lax.all_to_all(spread_rows(rows_packed, experts_live, capacity, SPLIT), '...  19.2 us
    all_to_all x1, starting transfers between devices, local(): lax.all_to_all(spread_rows(grad_packed, experts_live, capacity, SPLIT), '...  8.19 us
  transfers between devices with their start and end apart: 3, of which 3 were waited for; matrix products, arithmetic and copies ran while one was open for 1% of the time, Pallas kernels for 0%

commit v1 on v0

v1 whole, which is shorter than its diff:
```python
import jax
import jax.numpy as jnp
from jax import lax
from jax.experimental import pallas as pl
from jax.experimental.pallas import tpu as pltpu
from jax.sharding import PartitionSpec as P

CAP = 8
BLOCK = 2 * CAP
NZ, NX, NC = 8, 4, 2
EXPERTS = NZ * NX * NC // 4
SECTIONS = 16
FF_DEV = 192
D = 2048
HALF = D // 2
ORDER = (4, 5, 6, 7, 3, 2, 1, 0)
MESH = pl.DeviceIdType.MESH
F32, BF16 = jnp.float32, jnp.bfloat16


def flipped(z, m):
    out = 0
    for bit in (4, 2, 1):
        b = (z // bit) % 2
        out = out + bit * ((1 - b) if m & bit else b)
    return out


def kernel(
    ids_ref, probs_ref, rows_ref, grad_ref, gate_hbm, up_hbm, down_hbm, out_hbm,
    weights, packed, held, shares, from_core, for_x, from_x, returned, back, result, landed,
    load_sem, own_sem, to_sem, at_sem, core_send, core_recv, x_send, x_recv, cross_send, cross_recv,
    rc_send, rc_recv, rx_send, rx_recv, ret_send, ret_recv, ret_own, shift_send, shift_recv, out_sem,
):
    sec = lax.axis_index("section")
    dev = lax.axis_index("expert")
    z, x, c = dev // (NX * NC), (dev // NC) % NX, dev % NC

    def at(zz, xx, cc):
        return {"section": sec, "expert": zz * (NX * NC) + xx * NC + cc}

    other_core = at(z, x, 1 - c)
    other_chip = at(z, x + 1 - 2 * (x % 2), c)
    column = (x, NX - 1 - x)
    peers = [(h, m, at(flipped(z, m), column[h], c)) for h in range(2) for m in ORDER]
    ahead = {"section": (sec + SECTIONS - 1) % SECTIONS, "expert": dev}
    behind = {"section": (sec + 1) % SECTIONS, "expert": dev}

    loads = [
        pltpu.make_async_copy(src, weights.at[pl.ds(i * FF_DEV, FF_DEV)], load_sem.at[i])
        for i, src in enumerate((gate_hbm, up_hbm, down_hbm))
    ]
    for load in loads:
        load.start()

    barrier = pltpu.get_barrier_semaphore()
    partners = [p for h, m, p in peers if (h, m) != (0, 0)] + [other_core, other_chip, ahead, behind]
    for partner in partners:
        pl.semaphore_signal(barrier, inc=1, device_id=partner, device_id_type=MESH)

    ids = ids_ref[...]
    tokens = ids.shape[1]
    named = (lax.broadcasted_iota(jnp.int32, (EXPERTS, tokens), 0) == ids).astype(F32)
    before = (
        lax.broadcasted_iota(jnp.int32, (tokens, tokens), 0)
        < lax.broadcasted_iota(jnp.int32, (tokens, tokens), 1)
    ).astype(F32)
    earlier = jnp.dot(named, before, preferred_element_type=F32)
    rank = jnp.sum(earlier * named, axis=0, keepdims=True).astype(jnp.int32)
    message = jnp.where(ids % 2 == x // 2, 0, NZ) + jnp.bitwise_xor(ids // 2, z)
    place = message * BLOCK + rank
    row = lax.broadcasted_iota(jnp.int32, (EXPERTS * BLOCK, tokens), 0)
    pick = jnp.concatenate(
        [(row == place).astype(F32), (row == place + CAP).astype(F32)], axis=1
    ).astype(BF16)
    pair = jnp.concatenate([rows_ref[...], grad_ref[...]], axis=0)
    for n in range(0, D, 512):
        packed[:, :, n : n + 512] = (
            jnp.dot(pick, pair[:, n : n + 512], preferred_element_type=F32)
            .astype(BF16)
            .reshape(EXPERTS, BLOCK, 512)
        )

    pl.semaphore_wait(barrier, len(partners))

    sends = []
    for h, m, peer in peers:
        i = h * NZ + m
        if (h, m) == (0, 0):
            copy = pltpu.make_async_copy(packed.at[i], held.at[0, i], own_sem)
        else:
            copy = pltpu.make_async_remote_copy(
                src_ref=packed.at[i], dst_ref=held.at[0, i], send_sem=to_sem.at[i],
                recv_sem=at_sem.at[i], device_id=peer, device_id_type=MESH,
            )
        copy.start()
        sends.append((h, m, i, copy))

    for load in loads:
        load.wait()

    def forward(quarter, to, i, send, recv, device):
        return pltpu.make_async_remote_copy(
            src_ref=held.at[quarter, i], dst_ref=held.at[to, i], send_sem=send.at[i],
            recv_sem=recv.at[i], device_id=device, device_id_type=MESH,
        )

    def rows_of(h, first):
        block = held[:, h * NZ : (h + 1) * NZ, first : first + CAP, :]
        return block.reshape(4 * NZ * CAP, D)

    contract = (((1,), (1,)), ((), ()))
    chunk = NZ * CAP
    returns = []
    for h in range(2):
        mine = [s for s in sends if s[0] == h]
        on_core, on_x, on_cross = [], [], []
        for _, m, i, copy in mine:
            if (h, m) == (0, 0):
                copy.wait()
            else:
                copy.wait_recv()
            over = forward(0, 2, i, x_send, x_recv, other_chip)
            over.start()
            on_x.append(over)
            over = forward(0, 1, i, core_send, core_recv, other_core)
            over.start()
            on_core.append(over)
        for (_, m, i, _), over in zip(mine, on_x):
            over.wait_recv()
            cross = forward(2, 3, i, cross_send, cross_recv, other_core)
            cross.start()
            on_cross.append(cross)
        for over in on_core + on_cross:
            over.wait_recv()

        rows_in = rows_of(h, 0)
        rows_grad = rows_of(h, CAP)
        pre_gate = lax.dot_general(rows_in, weights[0:FF_DEV], contract, preferred_element_type=F32)
        pre_up = lax.dot_general(
            rows_in, weights[FF_DEV : 2 * FF_DEV], contract, preferred_element_type=F32
        )
        hidden = lax.dot_general(
            rows_grad, weights[2 * FF_DEV : 3 * FF_DEV], contract, preferred_element_type=F32
        )
        g = jax.nn.sigmoid(pre_gate)
        gate_coef = (hidden * pre_up * g * (1.0 + pre_gate * (1.0 - g))).astype(BF16)
        up_coef = (hidden * pre_gate * g).astype(BF16)
        for n in range(0, D, 512):
            total = jnp.dot(gate_coef, weights[0:FF_DEV, n : n + 512], preferred_element_type=F32)
            total = total + jnp.dot(
                up_coef, weights[FF_DEV : 2 * FF_DEV, n : n + 512], preferred_element_type=F32
            )
            shares[h, :, :, n : n + 512] = total.astype(BF16).reshape(4, chunk, 512)

        to_core = []
        for j, quarter in enumerate((3, 1)):
            copy = pltpu.make_async_remote_copy(
                src_ref=shares.at[h, quarter], dst_ref=from_core.at[h, j],
                send_sem=rc_send.at[h, j], recv_sem=rc_recv.at[h, j],
                device_id=other_core, device_id_type=MESH,
            )
            copy.start()
            to_core.append(copy)
        to_core[0].wait_recv()
        for_x[h] = (shares[h, 2].astype(F32) + from_core[h, 0].astype(F32)).astype(BF16)
        to_x = pltpu.make_async_remote_copy(
            src_ref=for_x.at[h], dst_ref=from_x.at[h], send_sem=rx_send.at[h],
            recv_sem=rx_recv.at[h], device_id=other_chip, device_id_type=MESH,
        )
        to_x.start()
        to_core[1].wait_recv()
        to_x.wait_recv()
        total = shares[h, 0].astype(F32) + from_core[h, 1].astype(F32) + from_x[h].astype(F32)
        total = total.astype(BF16).reshape(NZ, CAP, D)
        returned[h, :, 0:CAP, :] = total[:, :, 0:HALF]
        returned[h, :, CAP:BLOCK, :] = total[:, :, HALF:D]
        for _, m, peer in peers[h * NZ : (h + 1) * NZ]:
            if (h, m) == (0, 0):
                copy = pltpu.make_async_copy(returned.at[h, m], back.at[h, m], ret_own)
            else:
                copy = pltpu.make_async_remote_copy(
                    src_ref=returned.at[h, m], dst_ref=back.at[h, m],
                    send_sem=ret_send.at[h, m], recv_sem=ret_recv.at[h, m],
                    device_id=peer, device_id_type=MESH,
                )
            copy.start()
            returns.append((h, m, copy))
        for copy in to_core + [to_x] + on_core + on_x + on_cross:
            copy.wait_send()

    for h, m, copy in returns:
        if (h, m) == (0, 0):
            copy.wait()
        else:
            copy.wait_recv()

    eye = lax.broadcasted_iota(jnp.int32, (tokens, tokens), 0) == lax.broadcasted_iota(
        jnp.int32, (tokens, tokens), 1
    )
    place_col = jnp.sum(jnp.where(eye, place, 0), axis=1, keepdims=True)
    prob_col = jnp.sum(jnp.where(eye, probs_ref[...], 0.0), axis=1, keepdims=True)
    slot = lax.broadcasted_iota(jnp.int32, (tokens, EXPERTS * BLOCK), 1)
    rows_back = back[...].reshape(EXPERTS * BLOCK, HALF)
    for side in range(2):
        select = (slot == place_col + side * CAP).astype(BF16)
        own = jnp.dot(select, rows_back, preferred_element_type=F32)
        here = grad_ref[:, side * HALF : (side + 1) * HALF].astype(F32)
        result[side] = (here + prob_col * own).astype(BF16)
        shift = pltpu.make_async_remote_copy(
            src_ref=result.at[side], dst_ref=landed.at[side], send_sem=shift_send.at[side],
            recv_sem=shift_recv.at[side], device_id=ahead, device_id_type=MESH,
        )
        shift.start()
    outs = []
    for side in range(2):
        shift = pltpu.make_async_remote_copy(
            src_ref=result.at[side], dst_ref=landed.at[side], send_sem=shift_send.at[side],
            recv_sem=shift_recv.at[side], device_id=ahead, device_id_type=MESH,
        )
        shift.wait()
        out = pltpu.make_async_copy(
            landed.at[side], out_hbm.at[:, pl.ds(side * HALF, HALF)], out_sem.at[side]
        )
        out.start()
        outs.append(out)
    for h, m, i, copy in sends:
        if (h, m) != (0, 0):
            copy.wait_send()
    for h, m, copy in returns:
        if (h, m) != (0, 0):
            copy.wait_send()
    for out in outs:
        out.wait()


def local(route_ids, route_probs, checkpoints, grad_in, gate_weight, up_weight, down_weight):
    tokens = route_ids.shape[2]
    dma = pltpu.SemaphoreType.DMA
    vmem = pl.BlockSpec(memory_space=pltpu.VMEM)
    hbm = pl.BlockSpec(memory_space=pl.ANY)
    out = pl.pallas_call(
        kernel,
        out_shape=jax.ShapeDtypeStruct((tokens, D), BF16),
        in_specs=[vmem] * 4 + [hbm] * 3,
        out_specs=hbm,
        scratch_shapes=[
            pltpu.VMEM((3 * FF_DEV, D), BF16),
            pltpu.VMEM((EXPERTS, BLOCK, D), BF16),
            pltpu.VMEM((4, EXPERTS, BLOCK, D), BF16),
            pltpu.VMEM((2, 4, NZ * CAP, D), BF16),
            pltpu.VMEM((2, 2, NZ * CAP, D), BF16),
            pltpu.VMEM((2, NZ * CAP, D), BF16),
            pltpu.VMEM((2, NZ * CAP, D), BF16),
            pltpu.VMEM((2, NZ, BLOCK, HALF), BF16),
            pltpu.VMEM((2, NZ, BLOCK, HALF), BF16),
            pltpu.VMEM((2, tokens, HALF), BF16),
            pltpu.VMEM((2, tokens, HALF), BF16),
            dma((3,)), dma, dma((16,)), dma((16,)),
            dma((16,)), dma((16,)), dma((16,)), dma((16,)), dma((16,)), dma((16,)),
            dma((2, 2)), dma((2, 2)), dma((2,)), dma((2,)),
            dma((2, NZ)), dma((2, NZ)), dma, dma((2,)), dma((2,)), dma((2,)),
        ],
        compiler_params=pltpu.CompilerParams(
            collective_id=0, has_side_effects=True, vmem_limit_bytes=48 * 1024 * 1024
        ),
        cost_estimate=pl.CostEstimate(
            flops=2 * 512 * D * FF_DEV * 5, bytes_accessed=3 * 1024 * 1024, transcendentals=512 * FF_DEV
        ),
    )(
        route_ids.reshape(1, tokens),
        route_probs.reshape(1, tokens),
        checkpoints[0, 0],
        grad_in[0],
        jnp.swapaxes(gate_weight[0], 0, 1),
        jnp.swapaxes(up_weight[0], 0, 1),
        down_weight[0],
    )
    return out[None]


def solution(mesh):
    placed = (
        P(None, "section", "expert", None),
        P(None, "section", "expert", None),
        P(None, "section", "expert", None),
        P("section", "expert", None),
        P("section", None, "expert"),
        P("section", None, "expert"),
        P("section", "expert", None),
    )
    return jax.shard_map(
        local, mesh=mesh, in_specs=placed, out_specs=P("section", "expert", None), check_vma=False
    )
```

time: 382 us -> 143 us (0.37)
  the two profiles are of different devices: /device:TPU:60 before, /device:TPU:120 now
where the time goes in v1:
time: 143 us; the launch traced here: 142 us
  Pallas kernels  136 us (95%)
  local copies, waits for them, and re-layouts  6.67 us (5%)
    pallas_call x1, Pallas kernels, local(): pl.pallas_call(kernel, out_shape=jax.ShapeDtypeStruct((tokens, D), BF16),...  136 us
    unnamed x15, local copies, waits for them, and re-layouts  6.67 us

profile of v1, /device:TPU:120, one launch (start us, length us, event | category | flops | bytes accessed | tf_op | source)
XLA Modules:
  0.0 142.3 jit_solution(17153084781306318783)
XLA Ops:
  0.0 0.0 copy-start.5
  0.0 0.0 copy-start.6
  0.0 0.7 copy-done.5
  0.7 0.0 copy-done.6
  0.7 0.0 copy-start
  0.7 1.1 copy-done
  1.8 0.0 copy-start.1
  1.8 1.1 copy-done.1
  2.9 0.0 copy-start.2
  2.9 1.1 copy-done.2
  4.1 0.0 copy-start.3
  4.1 0.9 copy-done.3
  5.0 0.0 copy-start.4
  5.0 0.9 copy-done.4
  6.0 135.6 %shard_map.73 = bf16[64,2048]{1,0:T(8,128)(2,1)S(1)} custom-call(s32[1,64]{1,0:T(1,128)S(1)} %bitcast.18, f32[1,64]{1,0:T(1,128)S(1)} %bitcast.19, bf16[64,2048]{1,0:T(8,128)(2,1)S(1)} %bitcast.16, bf16[64,2048]{1,0:T(8,128)(2,1)S(1)} %bitcast.17, bf16[192,2048]{1,0:T(8,128)(2,1)S(1)} %bitcast.13, bf16[192,2048]{1,0:T(8,128)(2,1)S(1)} %bitcast.14, ...), custom_call_target="tpu_custom_call" | custom-call | flops 2013265920 | bytes 3145728 | tf_op jit(solution)/shard_map/pallas_call | solution.py:242
  141.6 0.7 copy.9
Async XLA Ops:
  0.0 0.7 copy-start.5
  0.0 0.7 copy-start.6
  0.7 1.1 copy-start
  1.8 1.1 copy-start.1
  2.9 1.1 copy-start.2
  4.1 0.9 copy-start.3
  5.0 0.9 copy-start.4

commit v2 on v1

v2 whole, which is shorter than its diff:
```python
import jax
import jax.numpy as jnp
from jax import lax
from jax.experimental import pallas as pl
from jax.experimental.pallas import tpu as pltpu
from jax.sharding import PartitionSpec as P

CAP = 8
BLOCK = 2 * CAP
NZ, NX, NC = 8, 4, 2
EXPERTS = NZ * NX * NC // 4
SECTIONS = 16
FF_DEV = 192
D = 2048
HALF = D // 2
QUAD = D // 4
NY = 8
PIECE = 16
CHUNKS = ((0, 4), (0, 0), (1, 0), (1, 4))
ORDER = (
    (0, 4), (0, 5), (0, 6), (0, 7), (1, 4), (0, 3), (0, 2), (1, 5),
    (0, 1), (0, 0), (1, 6), (1, 3), (1, 2), (1, 7), (1, 1), (1, 0),
)
WIDE = 4
CROWS = WIDE * CAP
MESH = pl.DeviceIdType.MESH
F32, BF16 = jnp.float32, jnp.bfloat16


def flipped(z, m):
    out = 0
    for bit in (4, 2, 1):
        b = (z // bit) % 2
        out = out + bit * ((1 - b) if m & bit else b)
    return out


def kernel(
    ids_ref, probs_ref, rows_hbm, grad_hbm, gate_hbm, up_hbm, down_hbm, out_hbm,
    weights, pair, packed, held, shares, from_core, for_x, from_x, returned, back, result, relay,
    load_sem, pair_sem, own_sem, to_sem, at_sem, x_send, x_recv, core_send, core_recv,
    rc_send, rc_recv, rx_send, rx_recv, ret_send, ret_recv, ret_own,
    shift_send, shift_recv, leg_send, leg_recv, end_send, end_recv,
):
    sec = lax.axis_index("section")
    dev = lax.axis_index("expert")
    z, x, c = dev // (NX * NC), (dev // NC) % NX, dev % NC
    y = sec % NY
    depth = (sec // NY) * NZ + z
    tokens = ids_ref.shape[1]

    def at(zz, xx, cc):
        return {"section": sec, "expert": zz * (NX * NC) + xx * NC + cc}

    def ring(yy, by):
        d = (depth + by + 2 * NZ) % (2 * NZ)
        return {
            "section": (d // NZ) * NY + yy,
            "expert": (d % NZ) * (NX * NC) + x * NC + c,
        }

    def remote(src, dst, send, recv, device):
        return pltpu.make_async_remote_copy(
            src_ref=src, dst_ref=dst, send_sem=send, recv_sem=recv,
            device_id=device, device_id_type=MESH,
        )

    other_core = at(z, x, 1 - c)
    other_chip = at(z, x + 1 - 2 * (x % 2), c)
    column = (x, NX - 1 - x)
    peers = {(h, m): at(flipped(z, m), column[h], c) for h, m in ORDER}
    ahead = {"section": (sec + SECTIONS - 1) % SECTIONS, "expert": dev}
    behind = {"section": (sec + 1) % SECTIONS, "expert": dev}
    first, last = y == 0, y == NY - 1
    edge = first | last

    barrier = pltpu.get_barrier_semaphore()

    def greet(device):
        pl.semaphore_signal(barrier, inc=1, device_id=device, device_id_type=MESH)

    partners = [peers[k] for k in ORDER if k != (0, 0)] + [other_core, other_chip]
    for partner in partners:
        greet(partner)

    @pl.when(y > 0)
    def _():
        greet(ahead)

    @pl.when(y < NY - 1)
    def _():
        greet(behind)

    @pl.when(edge)
    def _():
        for by in (1, -1):
            greet(ring(y, 7 * by))
            greet(ring(NY - 1 - y, by))

    takes = [
        pltpu.make_async_copy(src, pair.at[pl.ds(i * tokens, tokens)], pair_sem.at[i])
        for i, src in enumerate((rows_hbm, grad_hbm))
    ]
    loads = [
        pltpu.make_async_copy(src, weights.at[pl.ds(i * FF_DEV, FF_DEV)], load_sem.at[i])
        for i, src in enumerate((gate_hbm, up_hbm, down_hbm))
    ]
    for load in takes + loads:
        load.start()

    ids = ids_ref[...]
    named = (lax.broadcasted_iota(jnp.int32, (EXPERTS, tokens), 0) == ids).astype(F32)
    before = (
        lax.broadcasted_iota(jnp.int32, (tokens, tokens), 0)
        < lax.broadcasted_iota(jnp.int32, (tokens, tokens), 1)
    ).astype(F32)
    earlier = jnp.dot(named, before, preferred_element_type=F32)
    rank = jnp.sum(earlier * named, axis=0, keepdims=True).astype(jnp.int32)
    message = jnp.where(ids % 2 == x // 2, 0, NZ) + jnp.bitwise_xor(ids // 2, z)
    place = message * BLOCK + rank
    row = lax.broadcasted_iota(jnp.int32, (EXPERTS * BLOCK, tokens), 0)
    pick = jnp.concatenate(
        [(row == place).astype(F32), (row == place + CAP).astype(F32)], axis=1
    ).astype(BF16)
    for take in takes:
        take.wait()
    for n in range(0, D, QUAD):
        packed[:, :, n : n + QUAD] = (
            jnp.dot(pick, pair[:, n : n + QUAD], preferred_element_type=F32)
            .astype(BF16)
            .reshape(EXPERTS, BLOCK, QUAD)
        )

    @pl.when(edge)
    def _():
        pl.semaphore_wait(barrier, len(partners) + 5)

    @pl.when(jnp.logical_not(edge))
    def _():
        pl.semaphore_wait(barrier, len(partners) + 2)

    sends = {}
    for h, m in ORDER:
        i = h * NZ + m
        if i == 0:
            copy = pltpu.make_async_copy(packed.at[i], held.at[0, i], own_sem)
        else:
            copy = remote(packed.at[i], held.at[0, i], to_sem.at[i], at_sem.at[i], peers[h, m])
        copy.start()
        sends[i] = copy

    for load in loads:
        load.wait()

    contract = (((1,), (1,)), ((), ()))
    unsent = []

    def gather(k):
        h, m0 = CHUNKS[k]
        i0 = h * NZ + m0
        over_x = []
        for i in range(i0 + WIDE - 1, i0 - 1, -1) if m0 == 0 else range(i0, i0 + WIDE):
            if i == 0:
                sends[i].wait()
            else:
                sends[i].wait_recv()
            copy = remote(held.at[0, i], held.at[2, i], x_send.at[i], x_recv.at[i], other_chip)
            copy.start()
            over_x.append(copy)
        many = pl.ds(i0, WIDE)
        own = remote(held.at[0, many], held.at[1, many], core_send.at[k, 0], core_recv.at[k, 0], other_core)
        own.start()
        for copy in over_x:
            copy.wait_recv()
        cross = remote(held.at[2, many], held.at[3, many], core_send.at[k, 1], core_recv.at[k, 1], other_core)
        cross.start()
        own.wait_recv()
        cross.wait_recv()
        unsent.extend(over_x + [own, cross])

    def compute(k):
        h, m0 = CHUNKS[k]
        i0 = h * NZ + m0

        def rows_of(top):
            return held[:, i0 : i0 + WIDE, top : top + CAP, :].reshape(4 * CROWS, D)

        rows_in, rows_grad = rows_of(0), rows_of(CAP)
        pre_gate = lax.dot_general(rows_in, weights[0:FF_DEV], contract, preferred_element_type=F32)
        pre_up = lax.dot_general(
            rows_in, weights[FF_DEV : 2 * FF_DEV], contract, preferred_element_type=F32
        )
        hidden = lax.dot_general(
            rows_grad, weights[2 * FF_DEV : 3 * FF_DEV], contract, preferred_element_type=F32
        )
        g = jax.nn.sigmoid(pre_gate)
        gate_coef = (hidden * pre_up * g * (1.0 + pre_gate * (1.0 - g))).astype(BF16)
        up_coef = (hidden * pre_gate * g).astype(BF16)
        for n in range(0, D, QUAD):
            total = jnp.dot(gate_coef, weights[0:FF_DEV, n : n + QUAD], preferred_element_type=F32)
            total = total + jnp.dot(
                up_coef, weights[FF_DEV : 2 * FF_DEV, n : n + QUAD], preferred_element_type=F32
            )
            shares[k, :, :, n : n + QUAD] = total.astype(BF16).reshape(4, CROWS, QUAD)
        for j, quarter in enumerate((3, 1)):
            copy = to_core(k, j, quarter)
            copy.start()
            unsent.append(copy)

    def to_core(k, j, quarter):
        return remote(
            shares.at[k, quarter], from_core.at[k, j], rc_send.at[k, j], rc_recv.at[k, j], other_core
        )

    def to_chip(k):
        return remote(for_x.at[k], from_x.at[k], rx_send.at[k], rx_recv.at[k], other_chip)

    def reduce(k):
        to_core(k, 0, 3).wait_recv()
        for_x[k] = (shares[k, 2].astype(F32) + from_core[k, 0].astype(F32)).astype(BF16)
        copy = to_chip(k)
        copy.start()
        unsent.append(copy)

    returns = {}

    def give_back(k):
        h, m0 = CHUNKS[k]
        to_core(k, 1, 1).wait_recv()
        to_chip(k).wait_recv()
        for side in range(2):
            for half in range(2):
                n = side * HALF + half * QUAD
                total = (
                    shares[k, 0, :, n : n + QUAD].astype(F32)
                    + from_core[k, 1, :, n : n + QUAD].astype(F32)
                    + from_x[k, :, n : n + QUAD].astype(F32)
                )
                returned[side, k, :, half * CAP : (half + 1) * CAP, :] = total.astype(BF16).reshape(
                    WIDE, CAP, QUAD
                )
            for j in range(WIDE):
                m = m0 + j
                i = h * NZ + m
                src, dst = returned.at[side, k, j], back.at[side, i]
                if i == 0:
                    copy = pltpu.make_async_copy(src, dst, ret_own.at[side])
                else:
                    copy = remote(src, dst, ret_send.at[side, i], ret_recv.at[side, i], peers[h, m])
                copy.start()
                returns[side, i] = copy

    gather(0)
    compute(0)
    reduce(0)
    gather(1)
    give_back(0)
    compute(1)
    reduce(1)
    gather(2)
    give_back(1)
    compute(2)
    reduce(2)
    give_back(2)
    gather(3)
    compute(3)
    reduce(3)
    give_back(3)

    eye = lax.broadcasted_iota(jnp.int32, (tokens, tokens), 0) == lax.broadcasted_iota(
        jnp.int32, (tokens, tokens), 1
    )
    place_col = jnp.sum(jnp.where(eye, place, 0), axis=1, keepdims=True)
    prob_col = jnp.sum(jnp.where(eye, probs_ref[...], 0.0), axis=1, keepdims=True)
    slot = lax.broadcasted_iota(jnp.int32, (tokens, EXPERTS * BLOCK), 1)

    def piece(ref, side, p):
        return ref.at[pl.ds(p * PIECE, PIECE), pl.ds(side * HALF, HALF)]

    def whole(side):
        cols = pl.ds(side * HALF, HALF)
        return remote(
            result.at[:, cols], out_hbm.at[:, cols], shift_send.at[side], shift_recv.at[side], ahead
        )

    def leg(side, j, by, plane):
        p = 2 * plane + j
        way = ring(NY - 1, by) if plane else ring(0, 7 * by)
        return remote(
            piece(result, side, p), relay.at[side, j], leg_send.at[side, p], leg_recv.at[side, j], way
        )

    def end(side, j, by, plane):
        p = 2 * plane + j
        way = ring(NY - 1, 7 * by if plane else by)
        return remote(
            relay.at[side, j], piece(out_hbm, side, p), end_send.at[side, j], end_recv.at[side, p], way
        )

    ways = ((0, 1), (1, -1))

    def combine(side):
        for i in range(EXPERTS):
            if i == 0:
                returns[side, i].wait()
            else:
                returns[side, i].wait_recv()
        rows_back = back[side].reshape(EXPERTS * BLOCK, QUAD)
        for half in range(2):
            n = side * HALF + half * QUAD
            select = (slot == place_col + half * CAP).astype(BF16)
            own = jnp.dot(select, rows_back, preferred_element_type=F32)
            here = pair[tokens : 2 * tokens, n : n + QUAD].astype(F32)
            result[:, n : n + QUAD] = (here + prob_col * own).astype(BF16)

        @pl.when(jnp.logical_not(first))
        def _():
            whole(side).start()

        @pl.when(first)
        def _():
            for j, by in ways:
                for plane in range(2):
                    leg(side, j, by, plane).start()

    def pass_on(side, plane):
        for j, by in ways:
            leg(side, j, by, plane).wait_recv()
            end(side, j, by, plane).start()

    combine(0)

    @pl.when(last)
    def _():
        pass_on(0, 1)

    combine(1)

    @pl.when(first)
    def _():
        pass_on(0, 0)
        pass_on(1, 0)

    @pl.when(last)
    def _():
        pass_on(1, 1)

    @pl.when(jnp.logical_not(last))
    def _():
        for side in range(2):
            whole(side).wait_recv()

    @pl.when(last)
    def _():
        for side in range(2):
            for j, by in ways:
                for plane in range(2):
                    end(side, j, by, plane).wait_recv()

    @pl.when(jnp.logical_not(first))
    def _():
        for side in range(2):
            whole(side).wait_send()

    @pl.when(first)
    def _():
        for side in range(2):
            for j, by in ways:
                for plane in range(2):
                    leg(side, j, by, plane).wait_send()
                end(side, j, by, 0).wait_send()

    @pl.when(last)
    def _():
        for side in range(2):
            for j, by in ways:
                end(side, j, by, 1).wait_send()

    for copy in unsent:
        copy.wait_send()
    for i, copy in sends.items():
        if i:
            copy.wait_send()
    for (side, i), copy in returns.items():
        if i:
            copy.wait_send()


def local(route_ids, route_probs, checkpoints, grad_in, gate_weight, up_weight, down_weight):
    tokens = route_ids.shape[2]
    dma = pltpu.SemaphoreType.DMA
    vmem = pl.BlockSpec(memory_space=pltpu.VMEM)
    hbm = pl.BlockSpec(memory_space=pl.ANY)
    chunks = len(CHUNKS)
    out = pl.pallas_call(
        kernel,
        out_shape=jax.ShapeDtypeStruct((tokens, D), BF16),
        in_specs=[vmem] * 2 + [hbm] * 5,
        out_specs=hbm,
        scratch_shapes=[
            pltpu.VMEM((3 * FF_DEV, D), BF16),
            pltpu.VMEM((2 * tokens, D), BF16),
            pltpu.VMEM((EXPERTS, BLOCK, D), BF16),
            pltpu.VMEM((4, EXPERTS, BLOCK, D), BF16),
            pltpu.VMEM((chunks, 4, CROWS, D), BF16),
            pltpu.VMEM((chunks, 2, CROWS, D), BF16),
            pltpu.VMEM((chunks, CROWS, D), BF16),
            pltpu.VMEM((chunks, CROWS, D), BF16),
            pltpu.VMEM((2, chunks, WIDE, BLOCK, QUAD), BF16),
            pltpu.VMEM((2, EXPERTS, BLOCK, QUAD), BF16),
            pltpu.VMEM((tokens, D), BF16),
            pltpu.VMEM((2, 2, PIECE, HALF), BF16),
            dma((3,)), dma((2,)), dma, dma((16,)), dma((16,)), dma((16,)), dma((16,)),
            dma((chunks, 2)), dma((chunks, 2)), dma((chunks, 2)), dma((chunks, 2)),
            dma((chunks,)), dma((chunks,)), dma((2, 16)), dma((2, 16)), dma((2,)),
            dma((2,)), dma((2,)), dma((2, 4)), dma((2, 2)), dma((2, 2)), dma((2, 4)),
        ],
        compiler_params=pltpu.CompilerParams(
            collective_id=0, has_side_effects=True, vmem_limit_bytes=60 * 1024 * 1024
        ),
        cost_estimate=pl.CostEstimate(
            flops=2 * 512 * D * FF_DEV * 5, bytes_accessed=3 * 1024 * 1024, transcendentals=512 * FF_DEV
        ),
    )(
        route_ids.reshape(1, tokens),
        route_probs.reshape(1, tokens),
        checkpoints[0, 0],
        grad_in[0],
        jnp.swapaxes(gate_weight[0], 0, 1),
        jnp.swapaxes(up_weight[0], 0, 1),
        down_weight[0],
    )
    return out[None]


def solution(mesh):
    placed = (
        P(None, "section", "expert", None),
        P(None, "section", "expert", None),
        P(None, "section", "expert", None),
        P("section", "expert", None),
        P("section", None, "expert"),
        P("section", None, "expert"),
        P("section", "expert", None),
    )
    return jax.shard_map(
        local, mesh=mesh, in_specs=placed, out_specs=P("section", "expert", None), check_vma=False
    )
```

time: 143 us -> 143 us (level)
  the two profiles are of different devices: /device:TPU:120 before, /device:TPU:56 now
where the time goes in v2:
time: 143 us
  Pallas kernels  141 us (99%)
  local copies, waits for them, and re-layouts  1.67 us (1%)
    pallas_call x1, Pallas kernels, local(): pl.pallas_call(kernel, out_shape=jax.ShapeDtypeStruct((tokens, D), BF16),...  141 us

profile of v2, /device:TPU:56, one launch (start us, length us, event | category | flops | bytes accessed | tf_op | source)
XLA Modules:
  0.0 142.9 jit_solution(8200355988469287685)
XLA Ops:
  0.0 141.2 %shard_map.73 = bf16[64,2048]{1,0:T(8,128)(2,1)} custom-call(s32[1,64]{1,0:T(1,128)} %bitcast.18, f32[1,64]{1,0:T(1,128)} %bitcast.19, bf16[64,2048]{1,0:T(8,128)(2,1)} %bitcast.16, bf16[64,2048]{1,0:T(8,128)(2,1)} %bitcast.17, bf16[192,2048]{1,0:T(8,128)(2,1)} %bitcast.13, bf16[192,2048]{1,0:T(8,128)(2,1)} %bitcast.14, bf16[192,2048]{1,0:T(8,128)(2,1)} %bitcast.15), custom_call_target="tpu_custom_call" | custom-call | flops 2013265920 | bytes 3145728 | tf_op jit(solution)/shard_map/pallas_call | solution.py:395
  141.2 1.7 %copy.9 = bf16[1,64,2048]{2,1,0:T(8,128)(2,1)} copy(bf16[1,64,2048]{2,1,0:T(8,128)(2,1)} %bitcast.12) | data formatting | bytes 524288

commit v3 on v2

v3 whole, which is shorter than its diff:
```python
import jax
import jax.numpy as jnp
from jax import lax
from jax.experimental import pallas as pl
from jax.experimental.pallas import tpu as pltpu
from jax.sharding import PartitionSpec as P

CAP = 8
BLOCK = 2 * CAP
NZ, NX, NC = 8, 4, 2
EXPERTS = NZ * NX * NC // 4
SECTIONS = 16
FF_DEV = 192
D = 2048
HALF = D // 2
QUAD = D // 4
NY = 8
PIECE = 16
PLANES = (0, NY - 1, 1, NY - 2)
NEXT = 1
NEAR = (0, 8, 1, 9, 2, 10, 3, 11)
FAR = (4, 5, 6, 7, 12, 13, 14, 15)
WINDOW = 4
CHUNKS = ((0, 4), (8, 4), (4, 2), (6, 2), (12, 2), (14, 2))
MESH = pl.DeviceIdType.MESH
F32, BF16 = jnp.float32, jnp.bfloat16


def flipped(z, m):
    out = 0
    for bit in (4, 2, 1):
        b = (z // bit) % 2
        out = out + bit * ((1 - b) if m & bit else b)
    return out


def kernel(
    ids_ref, probs_ref, rows_hbm, grad_hbm, gate_hbm, up_hbm, down_hbm, out_hbm,
    weights, pair, packed, held, shares, from_core, for_x, from_x, returned, back, result, relay,
    load_sem, pair_sem, own_sem, to_sem, at_sem, x_send, x_recv, core_send, core_recv,
    rc_send, rc_recv, rx_send, rx_recv, ret_send, ret_recv, ret_own,
    shift_send, shift_recv, leg_send, leg_recv, end_send, end_recv,
):
    sec = lax.axis_index("section")
    dev = lax.axis_index("expert")
    z, x, c = dev // (NX * NC), (dev // NC) % NX, dev % NC
    y = sec % NY
    depth = (sec // NY) * NZ + z
    tokens = ids_ref.shape[1]

    def at(zz, xx, cc):
        return {"section": sec, "expert": zz * (NX * NC) + xx * NC + cc}

    def ring(yy, by):
        d = (depth + by + 2 * NZ) % (2 * NZ)
        return {
            "section": (d // NZ) * NY + yy,
            "expert": (d % NZ) * (NX * NC) + x * NC + c,
        }

    def remote(src, dst, send, recv, device):
        return pltpu.make_async_remote_copy(
            src_ref=src, dst_ref=dst, send_sem=send, recv_sem=recv,
            device_id=device, device_id_type=MESH,
        )

    other_core = at(z, x, 1 - c)
    other_chip = at(z, x + 1 - 2 * (x % 2), c)
    column = (x, NX - 1 - x)
    peers = [at(flipped(z, i % NZ), column[i // NZ], c) for i in range(EXPERTS)]
    ahead = {"section": (sec + SECTIONS - 1) % SECTIONS, "expert": dev}
    behind = {"section": (sec + 1) % SECTIONS, "expert": dev}
    first, last = y == 0, y == NY - 1
    edge = first | last
    relays = edge | (y == 1) | (y == NY - 2)

    barrier = pltpu.get_barrier_semaphore()

    def greet(device):
        pl.semaphore_signal(barrier, inc=1, device_id=device, device_id_type=MESH)

    partners = peers[1:] + [other_core, other_chip]
    for partner in partners:
        greet(partner)

    @pl.when(y > 0)
    def _():
        greet(ahead)

    @pl.when(y < NY - 1)
    def _():
        greet(behind)

    @pl.when(first)
    def _():
        for plane in PLANES:
            for by in (1, -1):
                greet(ring(plane, by * NEXT))

    @pl.when(relays)
    def _():
        for by in (1, -1):
            greet(ring(0, by * NEXT))
            greet(ring(NY - 1, by * (NZ - NEXT)))

    @pl.when(last)
    def _():
        for plane in PLANES:
            for by in (1, -1):
                greet(ring(plane, by * (NZ - NEXT)))

    takes = [
        pltpu.make_async_copy(src, pair.at[pl.ds(i * tokens, tokens)], pair_sem.at[i])
        for i, src in enumerate((rows_hbm, grad_hbm))
    ]
    loads = [
        pltpu.make_async_copy(src, weights.at[pl.ds(i * FF_DEV, FF_DEV)], load_sem.at[i])
        for i, src in enumerate((gate_hbm, up_hbm, down_hbm))
    ]
    for load in takes + loads:
        load.start()

    ids = ids_ref[...]
    named = (lax.broadcasted_iota(jnp.int32, (EXPERTS, tokens), 0) == ids).astype(F32)
    before = (
        lax.broadcasted_iota(jnp.int32, (tokens, tokens), 0)
        < lax.broadcasted_iota(jnp.int32, (tokens, tokens), 1)
    ).astype(F32)
    earlier = jnp.dot(named, before, preferred_element_type=F32)
    rank = jnp.sum(earlier * named, axis=0, keepdims=True).astype(jnp.int32)
    message = jnp.where(ids % 2 == x // 2, 0, NZ) + jnp.bitwise_xor(ids // 2, z)
    place = message * BLOCK + rank
    row = lax.broadcasted_iota(jnp.int32, (EXPERTS * BLOCK, tokens), 0)
    pick = jnp.concatenate(
        [(row == place).astype(F32), (row == place + CAP).astype(F32)], axis=1
    ).astype(BF16)
    for take in takes:
        take.wait()
    for n in range(0, D, QUAD):
        packed[:, :, n : n + QUAD] = (
            jnp.dot(pick, pair[:, n : n + QUAD], preferred_element_type=F32)
            .astype(BF16)
            .reshape(EXPERTS, BLOCK, QUAD)
        )

    pairs = 2 * len(PLANES)

    @pl.when(edge)
    def _():
        pl.semaphore_wait(barrier, len(partners) + pairs + 5)

    @pl.when(relays & jnp.logical_not(edge))
    def _():
        pl.semaphore_wait(barrier, len(partners) + 6)

    @pl.when(jnp.logical_not(relays))
    def _():
        pl.semaphore_wait(barrier, len(partners) + 2)

    sends = [pltpu.make_async_copy(packed.at[0], held.at[0, 0], own_sem)] + [
        remote(packed.at[i], held.at[0, i], to_sem.at[i], at_sem.at[i], peers[i])
        for i in range(1, EXPERTS)
    ]
    over_x = [
        remote(held.at[0, i], held.at[2, i], x_send.at[i], x_recv.at[i], other_chip)
        for i in range(EXPERTS)
    ]
    waiting = list(FAR)

    def send_far():
        if waiting:
            sends[waiting.pop(0)].start()

    for _ in range(WINDOW - 1):
        send_far()
    for i in NEAR:
        sends[i].start()

    for load in loads:
        load.wait()

    def arrive(i):
        if i == 0:
            sends[i].wait()
        else:
            sends[i].wait_recv()
        over_x[i].start()

    def to_core(k, j):
        first_slot, slots = CHUNKS[k]
        many = pl.ds(first_slot, slots)
        return remote(
            held.at[2 * j, many], held.at[2 * j + 1, many], core_send.at[k, j], core_recv.at[k, j], other_core
        )

    def gather(k):
        first_slot, slots = CHUNKS[k]
        for i in range(first_slot, first_slot + slots):
            over_x[i].wait_recv()
        to_core(k, 1).start()
        to_core(k, 0).wait_recv()
        to_core(k, 1).wait_recv()

    contract = (((1,), (1,)), ((), ()))

    def rows_of_chunk(k):
        first_slot, slots = CHUNKS[k]
        return pl.ds(first_slot * CAP, slots * CAP)

    def share_to_core(k, j):
        rows = rows_of_chunk(k)
        return remote(
            shares.at[3 - 2 * j, rows], from_core.at[j, rows], rc_send.at[k, j], rc_recv.at[k, j], other_core
        )

    def sum_to_chip(k):
        rows = rows_of_chunk(k)
        return remote(for_x.at[rows], from_x.at[rows], rx_send.at[k], rx_recv.at[k], other_chip)

    def compute(k):
        first_slot, slots = CHUNKS[k]
        rows = rows_of_chunk(k)

        def rows_of(top):
            block = held[:, first_slot : first_slot + slots, top : top + CAP, :]
            return block.reshape(4 * slots * CAP, D)

        rows_in, rows_grad = rows_of(0), rows_of(CAP)
        pre_gate = lax.dot_general(rows_in, weights[0:FF_DEV], contract, preferred_element_type=F32)
        pre_up = lax.dot_general(
            rows_in, weights[FF_DEV : 2 * FF_DEV], contract, preferred_element_type=F32
        )
        hidden = lax.dot_general(
            rows_grad, weights[2 * FF_DEV : 3 * FF_DEV], contract, preferred_element_type=F32
        )
        g = jax.nn.sigmoid(pre_gate)
        gate_coef = (hidden * pre_up * g * (1.0 + pre_gate * (1.0 - g))).astype(BF16)
        up_coef = (hidden * pre_gate * g).astype(BF16)
        for n in range(0, D, QUAD):
            total = jnp.dot(gate_coef, weights[0:FF_DEV, n : n + QUAD], preferred_element_type=F32)
            total = total + jnp.dot(
                up_coef, weights[FF_DEV : 2 * FF_DEV, n : n + QUAD], preferred_element_type=F32
            )
            shares[:, rows, n : n + QUAD] = total.astype(BF16).reshape(4, slots * CAP, QUAD)
        for j in range(2):
            share_to_core(k, j).start()

    def reduce(k):
        rows = rows_of_chunk(k)
        share_to_core(k, 0).wait_recv()
        for_x[rows] = (shares[2, rows].astype(F32) + from_core[0, rows].astype(F32)).astype(BF16)
        sum_to_chip(k).start()

    def finish(k):
        first_slot, slots = CHUNKS[k]
        rows = rows_of_chunk(k)
        share_to_core(k, 1).wait_recv()
        sum_to_chip(k).wait_recv()
        for q in range(4):
            cols = slice(q * QUAD, (q + 1) * QUAD)
            total = (
                shares[0, rows, cols].astype(F32)
                + from_core[1, rows, cols].astype(F32)
                + from_x[rows, cols].astype(F32)
            )
            top = q % 2 * CAP
            returned[q // 2, first_slot : first_slot + slots, top : top + CAP, :] = total.astype(
                BF16
            ).reshape(slots, CAP, QUAD)

    def one_back(side, i):
        src, dst = returned.at[side, i], back.at[side, i]
        if i == 0:
            return pltpu.make_async_copy(src, dst, ret_own.at[side])
        return remote(src, dst, ret_send.at[side, i], ret_recv.at[side, i], peers[i])

    def give_back(side, k):
        first_slot, slots = CHUNKS[k]
        for i in range(first_slot, first_slot + slots):
            one_back(side, i).start()

    for i in NEAR[0::2]:
        arrive(i)
    to_core(0, 0).start()
    send_far()
    for i in NEAR[1::2]:
        arrive(i)
    to_core(1, 0).start()
    gather(0)
    compute(0)
    gather(1)
    compute(1)
    for k in range(2, 6):
        first_slot, slots = CHUNKS[k]
        for i in range(first_slot, first_slot + slots):
            arrive(i)
            if waiting:
                sends[i].wait_send()
                send_far()
        to_core(k, 0).start()
        if k == 2:
            reduce(0)
            reduce(1)
        else:
            reduce(k - 1)
        if k == 5:
            for n in (2, 3):
                give_back(0, n)
        gather(k)
        compute(k)
        if k == 3:
            for n in (0, 1):
                finish(n)
                for side in range(2):
                    give_back(side, n)
            finish(2)
        if k == 4:
            finish(3)
    finish(4)
    give_back(0, 4)
    reduce(5)
    finish(5)
    give_back(0, 5)
    give_back(1, 2)
    for i in (14, 15):
        one_back(0, i).wait_send()
    for k in (3, 4, 5):
        give_back(1, k)

    eye = lax.broadcasted_iota(jnp.int32, (tokens, tokens), 0) == lax.broadcasted_iota(
        jnp.int32, (tokens, tokens), 1
    )
    place_col = jnp.sum(jnp.where(eye, place, 0), axis=1, keepdims=True)
    prob_col = jnp.sum(jnp.where(eye, probs_ref[...], 0.0), axis=1, keepdims=True)
    slot = lax.broadcasted_iota(jnp.int32, (tokens, EXPERTS * BLOCK), 1)

    def piece(ref, side, p):
        return ref.at[pl.ds(p % 4 * PIECE, PIECE), pl.ds(side * HALF + p // 4 * QUAD, QUAD)]

    def whole(side):
        cols = pl.ds(side * HALF, HALF)
        return remote(
            result.at[:, cols], out_hbm.at[:, cols], shift_send.at[side], shift_recv.at[side], ahead
        )

    def leg(side, n, j, by):
        p = 2 * n + j
        return remote(
            piece(result, side, p), relay.at[side, j], leg_send.at[side, p], leg_recv.at[side, j],
            ring(PLANES[n], by * NEXT),
        )

    def end(side, n, j, by):
        p = 2 * n + j
        return remote(
            relay.at[side, j], piece(out_hbm, side, p), end_send.at[side, j], end_recv.at[side, p],
            ring(NY - 1, by * (NZ - NEXT)),
        )

    ways = ((0, 1), (1, -1))

    def combine(side):
        for i in range(EXPERTS):
            if i == 0:
                one_back(side, i).wait()
            else:
                one_back(side, i).wait_recv()
        rows_back = back[side].reshape(EXPERTS * BLOCK, QUAD)
        for half in range(2):
            n = side * HALF + half * QUAD
            select = (slot == place_col + half * CAP).astype(BF16)
            own = jnp.dot(select, rows_back, preferred_element_type=F32)
            here = pair[tokens : 2 * tokens, n : n + QUAD].astype(F32)
            result[:, n : n + QUAD] = (here + prob_col * own).astype(BF16)

        @pl.when(jnp.logical_not(first))
        def _():
            whole(side).start()

        @pl.when(first)
        def _():
            for j, by in ways:
                for n in range(len(PLANES)):
                    leg(side, n, j, by).start()

    def pass_on(side):
        for n, plane in enumerate(PLANES):

            @pl.when(y == plane)
            def _():
                for j, by in ways:
                    leg(side, n, j, by).wait_recv()
                    end(side, n, j, by).start()

    combine(0)
    pass_on(0)
    combine(1)
    pass_on(1)

    @pl.when(jnp.logical_not(last))
    def _():
        for side in range(2):
            whole(side).wait_recv()

    @pl.when(last)
    def _():
        for side in range(2):
            for j, by in ways:
                for n in range(len(PLANES)):
                    end(side, n, j, by).wait_recv()

    @pl.when(jnp.logical_not(first))
    def _():
        for side in range(2):
            whole(side).wait_send()

    @pl.when(first)
    def _():
        for side in range(2):
            for j, by in ways:
                for n in range(len(PLANES)):
                    leg(side, n, j, by).wait_send()

    @pl.when(relays)
    def _():
        for side in range(2):
            for j, by in ways:
                end(side, 0, j, by).wait_send()

    for k, (first_slot, slots) in enumerate(CHUNKS):
        for j in range(2):
            to_core(k, j).wait_send()
            share_to_core(k, j).wait_send()
        sum_to_chip(k).wait_send()
    for i in range(EXPERTS):
        over_x[i].wait_send()
        if i and not (i in FAR and FAR.index(i) < EXPERTS // 2 - WINDOW):
            sends[i].wait_send()
        for side in range(2):
            if i and not (side == 0 and i in (14, 15)):
                one_back(side, i).wait_send()


def local(route_ids, route_probs, checkpoints, grad_in, gate_weight, up_weight, down_weight):
    tokens = route_ids.shape[2]
    dma = pltpu.SemaphoreType.DMA
    vmem = pl.BlockSpec(memory_space=pltpu.VMEM)
    hbm = pl.BlockSpec(memory_space=pl.ANY)
    chunks = len(CHUNKS)
    out = pl.pallas_call(
        kernel,
        out_shape=jax.ShapeDtypeStruct((tokens, D), BF16),
        in_specs=[vmem] * 2 + [hbm] * 5,
        out_specs=hbm,
        scratch_shapes=[
            pltpu.VMEM((3 * FF_DEV, D), BF16),
            pltpu.VMEM((2 * tokens, D), BF16),
            pltpu.VMEM((EXPERTS, BLOCK, D), BF16),
            pltpu.VMEM((4, EXPERTS, BLOCK, D), BF16),
            pltpu.VMEM((4, EXPERTS * CAP, D), BF16),
            pltpu.VMEM((2, EXPERTS * CAP, D), BF16),
            pltpu.VMEM((EXPERTS * CAP, D), BF16),
            pltpu.VMEM((EXPERTS * CAP, D), BF16),
            pltpu.VMEM((2, EXPERTS, BLOCK, QUAD), BF16),
            pltpu.VMEM((2, EXPERTS, BLOCK, QUAD), BF16),
            pltpu.VMEM((tokens, D), BF16),
            pltpu.VMEM((2, 2, PIECE, QUAD), BF16),
            dma((3,)), dma((2,)), dma, dma((16,)), dma((16,)), dma((16,)), dma((16,)),
            dma((chunks, 2)), dma((chunks, 2)), dma((chunks, 2)), dma((chunks, 2)),
            dma((chunks,)), dma((chunks,)), dma((2, 16)), dma((2, 16)), dma((2,)),
            dma((2,)), dma((2,)), dma((2, 8)), dma((2, 2)), dma((2, 2)), dma((2, 8)),
        ],
        compiler_params=pltpu.CompilerParams(
            collective_id=0, has_side_effects=True, vmem_limit_bytes=60 * 1024 * 1024
        ),
        cost_estimate=pl.CostEstimate(
            flops=2 * 512 * D * FF_DEV * 5, bytes_accessed=3 * 1024 * 1024, transcendentals=512 * FF_DEV
        ),
    )(
        route_ids.reshape(1, tokens),
        route_probs.reshape(1, tokens),
        checkpoints[0, 0],
        grad_in[0],
        jnp.swapaxes(gate_weight[0], 0, 1),
        jnp.swapaxes(up_weight[0], 0, 1),
        down_weight[0],
    )
    return out[None]


def solution(mesh):
    placed = (
        P(None, "section", "expert", None),
        P(None, "section", "expert", None),
        P(None, "section", "expert", None),
        P("section", "expert", None),
        P("section", None, "expert"),
        P("section", None, "expert"),
        P("section", "expert", None),
    )
    return jax.shard_map(
        local, mesh=mesh, in_specs=placed, out_specs=P("section", "expert", None), check_vma=False
    )
```

time: 143 us -> 128 us (0.90)
  Pallas kernels: 141 us -> 126 us
    pallas_call x1, Pallas kernels: 141 us -> 126 us  [local(): pl.pallas_call(kernel, out_shape=jax.ShapeDtypeStruct((tokens, D), BF16),...]
where the time goes in v3:
time: 128 us
  Pallas kernels  126 us (98%)
  local copies, waits for them, and re-layouts  1.67 us (1%)
    pallas_call x1, Pallas kernels, local(): pl.pallas_call(kernel, out_shape=jax.ShapeDtypeStruct((tokens, D), BF16),...  126 us

profile of v3, /device:TPU:56, one launch (start us, length us, event | category | flops | bytes accessed | tf_op | source)
XLA Modules:
  0.0 128.1 jit_solution(1520380616066521402)
XLA Ops:
  0.0 126.4 %shard_map.73 = bf16[64,2048]{1,0:T(8,128)(2,1)} custom-call(s32[1,64]{1,0:T(1,128)} %bitcast.18, f32[1,64]{1,0:T(1,128)} %bitcast.19, bf16[64,2048]{1,0:T(8,128)(2,1)} %bitcast.16, bf16[64,2048]{1,0:T(8,128)(2,1)} %bitcast.17, bf16[192,2048]{1,0:T(8,128)(2,1)} %bitcast.13, bf16[192,2048]{1,0:T(8,128)(2,1)} %bitcast.14, bf16[192,2048]{1,0:T(8,128)(2,1)} %bitcast.15), custom_call_target="tpu_custom_call" | custom-call | flops 2013265920 | bytes 3145728 | tf_op jit(solution)/shard_map/pallas_call | solution.py:450
  126.4 1.7 %copy.9 = bf16[1,64,2048]{2,1,0:T(8,128)(2,1)} copy(bf16[1,64,2048]{2,1,0:T(8,128)(2,1)} %bitcast.12) | data formatting | bytes 524288

commit v4 on v3

--- a/solution.py
+++ b/solution.py
@@ -20,7 +20,7 @@
 NEXT = 1
 NEAR = (0, 8, 1, 9, 2, 10, 3, 11)
 FAR = (4, 5, 6, 7, 12, 13, 14, 15)
-WINDOW = 4
+WINDOW = 5
 CHUNKS = ((0, 4), (8, 4), (4, 2), (6, 2), (12, 2), (14, 2))
 MESH = pl.DeviceIdType.MESH
 F32, BF16 = jnp.float32, jnp.bfloat16
@@ -307,6 +307,9 @@
             for n in (2, 3):
                 give_back(0, n)
         gather(k)
+        if k == 5:
+            for n in (2, 3):
+                give_back(1, n)
         compute(k)
         if k == 3:
             for n in (0, 1):
@@ -318,14 +321,11 @@
             finish(3)
     finish(4)
     give_back(0, 4)
+    give_back(1, 4)
     reduce(5)
     finish(5)
     give_back(0, 5)
-    give_back(1, 2)
-    for i in (14, 15):
-        one_back(0, i).wait_send()
-    for k in (3, 4, 5):
-        give_back(1, k)
+    give_back(1, 5)
 
     eye = lax.broadcasted_iota(jnp.int32, (tokens, tokens), 0) == lax.broadcasted_iota(
         jnp.int32, (tokens, tokens), 1
@@ -383,8 +383,9 @@
                 for n in range(len(PLANES)):
                     leg(side, n, j, by).start()
 
-    def pass_on(side):
-        for n, plane in enumerate(PLANES):
+    def pass_on(side, planes):
+        for plane in planes:
+            n = PLANES.index(plane)
 
             @pl.when(y == plane)
             def _():
@@ -393,9 +394,10 @@
                     end(side, n, j, by).start()
 
     combine(0)
-    pass_on(0)
+    pass_on(0, PLANES[1:])
     combine(1)
-    pass_on(1)
+    pass_on(0, PLANES[:1])
+    pass_on(1, PLANES)
 
     @pl.when(jnp.logical_not(last))
     def _():
@@ -437,7 +439,7 @@
         if i and not (i in FAR and FAR.index(i) < EXPERTS // 2 - WINDOW):
             sends[i].wait_send()
         for side in range(2):
-            if i and not (side == 0 and i in (14, 15)):
+            if i:
                 one_back(side, i).wait_send()
 
 

time: 128 us -> 126 us (0.984)
  Pallas kernels: 126 us -> 124 us
    pallas_call x1, Pallas kernels: 126 us -> 124 us  [local(): pl.pallas_call(kernel, out_shape=jax.ShapeDtypeStruct((tokens, D), BF16),...]
where the time goes in v4:
time: 126 us; the launch traced here: 125 us
  Pallas kernels  124 us (98%)
  local copies, waits for them, and re-layouts  1.67 us (1%)
    pallas_call x1, Pallas kernels, local(): pl.pallas_call(kernel, out_shape=jax.ShapeDtypeStruct((tokens, D), BF16),...  124 us

profile of v4, /device:TPU:56, one launch (start us, length us, event | category | flops | bytes accessed | tf_op | source)
XLA Modules:
  0.0 125.3 jit_solution(12613893331407440593)
XLA Ops:
  0.0 123.6 %shard_map.73 = bf16[64,2048]{1,0:T(8,128)(2,1)} custom-call(s32[1,64]{1,0:T(1,128)} %bitcast.18, f32[1,64]{1,0:T(1,128)} %bitcast.19, bf16[64,2048]{1,0:T(8,128)(2,1)} %bitcast.16, bf16[64,2048]{1,0:T(8,128)(2,1)} %bitcast.17, bf16[192,2048]{1,0:T(8,128)(2,1)} %bitcast.13, bf16[192,2048]{1,0:T(8,128)(2,1)} %bitcast.14, bf16[192,2048]{1,0:T(8,128)(2,1)} %bitcast.15), custom_call_target="tpu_custom_call" | custom-call | flops 2013265920 | bytes 3145728 | tf_op jit(solution)/shard_map/pallas_call | solution.py:452
  123.6 1.7 %copy.9 = bf16[1,64,2048]{2,1,0:T(8,128)(2,1)} copy(bf16[1,64,2048]{2,1,0:T(8,128)(2,1)} %bitcast.12) | data formatting | bytes 524288

commit v5 on v4

--- a/solution.py
+++ b/solution.py
@@ -290,7 +290,7 @@
     compute(0)
     gather(1)
     compute(1)
-    for k in range(2, 6):
+    def far(k):
         first_slot, slots = CHUNKS[k]
         for i in range(first_slot, first_slot + slots):
             arrive(i)
@@ -298,34 +298,41 @@
                 sends[i].wait_send()
                 send_far()
         to_core(k, 0).start()
-        if k == 2:
-            reduce(0)
-            reduce(1)
-        else:
-            reduce(k - 1)
-        if k == 5:
-            for n in (2, 3):
-                give_back(0, n)
-        gather(k)
-        if k == 5:
-            for n in (2, 3):
-                give_back(1, n)
-        compute(k)
-        if k == 3:
-            for n in (0, 1):
-                finish(n)
-                for side in range(2):
-                    give_back(side, n)
-            finish(2)
-        if k == 4:
-            finish(3)
+
+    far(2)
+    reduce(0)
+    reduce(1)
+    far(3)
+    gather(2)
+    compute(2)
+    for n in (0, 1):
+        finish(n)
+        for side in range(2):
+            give_back(side, n)
+    far(4)
+    reduce(2)
+    gather(3)
+    compute(3)
+    finish(2)
+    far(5)
+    give_back(0, 2)
+    reduce(3)
+    gather(4)
+    compute(4)
+    finish(3)
+    give_back(0, 3)
+    gather(5)
+    compute(5)
+    give_back(1, 2)
+    reduce(4)
+    give_back(1, 3)
+    reduce(5)
     finish(4)
-    give_back(0, 4)
-    give_back(1, 4)
-    reduce(5)
+    for side in range(2):
+        give_back(side, 4)
     finish(5)
-    give_back(0, 5)
-    give_back(1, 5)
+    for side in range(2):
+        give_back(side, 5)
 
     eye = lax.broadcasted_iota(jnp.int32, (tokens, tokens), 0) == lax.broadcasted_iota(
         jnp.int32, (tokens, tokens), 1

time: 126 us -> 123 us (0.976)
  Pallas kernels: 124 us -> 121 us
    pallas_call x1, Pallas kernels: 124 us -> 121 us  [local(): pl.pallas_call(kernel, out_shape=jax.ShapeDtypeStruct((tokens, D), BF16),...]
where the time goes in v5:
time: 123 us
  Pallas kernels  121 us (98%)
  local copies, waits for them, and re-layouts  1.67 us (1%)
    pallas_call x1, Pallas kernels, local(): pl.pallas_call(kernel, out_shape=jax.ShapeDtypeStruct((tokens, D), BF16),...  121 us

profile of v5, /device:TPU:56, one launch (start us, length us, event | category | flops | bytes accessed | tf_op | source)
XLA Modules:
  0.0 123.1 jit_solution(12314987676318053295)
XLA Ops:
  0.0 121.4 %shard_map.73 = bf16[64,2048]{1,0:T(8,128)(2,1)} custom-call(s32[1,64]{1,0:T(1,128)} %bitcast.18, f32[1,64]{1,0:T(1,128)} %bitcast.19, bf16[64,2048]{1,0:T(8,128)(2,1)} %bitcast.16, bf16[64,2048]{1,0:T(8,128)(2,1)} %bitcast.17, bf16[192,2048]{1,0:T(8,128)(2,1)} %bitcast.13, bf16[192,2048]{1,0:T(8,128)(2,1)} %bitcast.14, bf16[192,2048]{1,0:T(8,128)(2,1)} %bitcast.15), custom_call_target="tpu_custom_call" | custom-call | flops 2013265920 | bytes 3145728 | tf_op jit(solution)/shard_map/pallas_call | solution.py:459
  121.4 1.7 %copy.9 = bf16[1,64,2048]{2,1,0:T(8,128)(2,1)} copy(bf16[1,64,2048]{2,1,0:T(8,128)(2,1)} %bitcast.12) | data formatting | bytes 524288
